TPU v7x, 512 devices: a whole 4x4x16 slice. The times are simulated.
512 devices in a mesh: gx: 32 (over x, y, core), gy: 16 (over z).
Axes of the slice: x: 4, y: 4, z: 16, core: 2. Of those that a mesh axis runs over, the one named last changes fastest.
Arguments:
- right_side: float32 [2, 512, 2048], P(None, 'gx', 'gy'), may hold values from -160 to 160
- conductivity: float32 [512, 2048], P('gx', 'gy'), may hold values from 0.2 to 5
- leaf_inverse: float32 [128, 64, 128, 128], P('gx', 'gy'), may hold values from -1 to 4, as said below
- front_basis: float32 [512, 2048, 128], P('gx', 'gy'), may hold values from -0.25 to 0.25
- leaf_transfer: float32 [32, 16, 128, 128], P('gx', 'gy'), may hold values from -0.4375 to 0.4375
- node_transfer: float32 [32, 16, 8, 128, 128], P('gx', 'gy'), may hold values from -1 to 1, as said below
- leaf_front: float32 [32, 16, 128, 128], P('gx', 'gy'), may hold values from -1 to 1, as said below
- node_front: float32 [32, 16, 9, 128, 128], P('gx', 'gy'), may hold values from -1 to 1, as said below
Outputs:
- solution: float32 [2, 512, 2048], P(None, 'gx', 'gy')
- residual: float32 [2, 512, 2048], P(None, 'gx', 'gy')
- direction: float32 [2, 512, 2048], P(None, 'gx', 'gy')
Inputs may be any that keep to these rules, and one draw needn't show every extreme that they name: `leaf_inverse`: every block is symmetric and positive definite. `leaf_front`: every matrix is symmetric and positive definite. `node_front`: every matrix is symmetric and positive definite; entry h - 1 is the same for all tiles covered by one node of level h. `node_transfer`: entry h - 1 is the same for all tiles covered by one node of level h.
All inputs are finite; a program needn't handle non-finite values.
Results may differ from a plain program's by a relative error of at most 0.0001.
Values sent between devices are 32-bit elements; how exact they have to be, the bound alone decides.
A program may use at most 64 MiB of HBM per device.

v0:
```python
from functools import partial
import jax
import jax.numpy as jnp
from jax import lax
from jax.sharding import PartitionSpec as P

LBX = 4
LBY = 32
HIGHEST = lax.Precision.HIGHEST


def extended(cells, sides, width):
    for axis, dim in sides:
        count = lax.axis_size(axis)
        ends = count - 1
        head = lax.slice_in_dim(cells, 0, width, axis=dim)
        tail = lax.slice_in_dim(cells, cells.shape[dim] - width, cells.shape[dim], axis=dim)
        cells = jnp.concatenate(
            [
                lax.ppermute(tail, axis, [(i, (i + 1) % count) for i in range(ends)]),
                cells,
                lax.ppermute(head, axis, [((i + 1) % count, i) for i in range(ends)]),
            ],
            axis=dim,
        )
    return cells


def from_partner(value, axis, distance):
    mask = 2**distance
    pairs = [(source, source ^ mask) for source in range(lax.axis_size(axis))]
    return lax.ppermute(value, axis, pairs)


def operate_padded(padded, padded_k):
    extent_x = padded.shape[1] - 2
    extent_y = padded.shape[2] - 2
    center = padded[:, 1:-1, 1:-1]
    center_k = padded_k[1:-1, 1:-1]
    summed = jnp.zeros_like(center)
    for offset_x, offset_y in ((2, 1), (0, 1), (1, 2), (1, 0)):
        beside = padded[:, offset_x : offset_x + extent_x, offset_y : offset_y + extent_y]
        beside_k = padded_k[offset_x : offset_x + extent_x, offset_y : offset_y + extent_y]
        summed = summed + 0.5 * (center_k + beside_k) * (center - beside)
    return summed


def stencil(values, conductivity):
    stacked = jnp.concatenate([values, conductivity[None]], axis=0)
    padded = extended(stacked, (("gx", 1), ("gy", 2)), 1)
    return operate_padded(padded[:-1], padded[-1])


def leaf_apply(values, leaf_inverse):
    count_s, extent_x, extent_y = values.shape
    blocks_x = extent_x // LBX
    blocks_y = extent_y // LBY
    grouped = values.reshape(count_s, blocks_x, LBX, blocks_y, LBY).transpose(0, 1, 3, 2, 4)
    grouped = grouped.reshape(count_s, blocks_x, blocks_y, LBX * LBY)
    mapped = jnp.einsum("xyij,sxyj->sxyi", leaf_inverse, grouped, precision=HIGHEST)
    mapped = mapped.reshape(count_s, blocks_x, blocks_y, LBX, LBY).transpose(0, 1, 3, 2, 4)
    return mapped.reshape(count_s, extent_x, extent_y)


def spread_tree(coeffs, leaf_transfer, node_transfer, leaf_front, node_front):
    levels = lax.axis_size(("gx", "gy")).bit_length() - 1
    leaf_t = leaf_transfer[0, 0]
    leaf_f = leaf_front[0, 0]
    node_t = node_transfer[0, 0]
    node_f = node_front[0, 0]
    uppers = [coeffs]
    moving = jnp.dot(coeffs, leaf_t, precision=HIGHEST)
    for height in range(1, levels + 1):
        partner = from_partner(moving, ("gx", "gy"), height - 1)
        summed = moving + partner
        uppers.append(summed)
        if height < levels:
            moving = jnp.dot(summed, node_t[height - 1], precision=HIGHEST)
    downward = jnp.dot(uppers[levels], node_f[levels - 1], precision=HIGHEST)
    for height in range(levels, 1, -1):
        downward = jnp.dot(downward, node_t[height - 2].T, precision=HIGHEST) + jnp.dot(
            uppers[height - 1], node_f[height - 2], precision=HIGHEST
        )
    return jnp.dot(downward, leaf_t.T, precision=HIGHEST) + jnp.dot(
        coeffs, leaf_f, precision=HIGHEST
    )


def precondition(
    values, leaf_inverse, front_basis, leaf_transfer, node_transfer, leaf_front, node_front
):
    near = leaf_apply(values, leaf_inverse)
    coeffs = jnp.einsum("sab,abk->sk", values, front_basis, precision=HIGHEST)
    spread = spread_tree(coeffs, leaf_transfer, node_transfer, leaf_front, node_front)
    return near + jnp.einsum("sk,abk->sab", spread, front_basis, precision=HIGHEST)


def on_device(
    right_side,
    conductivity,
    leaf_inverse,
    front_basis,
    leaf_transfer,
    node_transfer,
    leaf_front,
    node_front,
):
    apply_inverse = partial(
        precondition,
        leaf_inverse=leaf_inverse,
        front_basis=front_basis,
        leaf_transfer=leaf_transfer,
        node_transfer=node_transfer,
        leaf_front=leaf_front,
        node_front=node_front,
    )
    first_z = apply_inverse(right_side)
    local_rz = jnp.sum(right_side * first_z, axis=(1, 2))
    rz_old = lax.psum(local_rz, ("gx", "gy"))
    applied = stencil(first_z, conductivity)
    curvature = lax.psum(jnp.sum(first_z * applied, axis=(1, 2)), ("gx", "gy"))
    step_size = (rz_old / curvature)[:, None, None]
    solution = step_size * first_z
    residual = right_side - step_size * applied
    second_z = apply_inverse(residual)
    rz_new = lax.psum(jnp.sum(residual * second_z, axis=(1, 2)), ("gx", "gy"))
    direction = second_z + (rz_new / rz_old)[:, None, None] * first_z
    return (solution, residual, direction)


def solution(mesh):
    return jax.shard_map(
        on_device,
        mesh=mesh,
        in_specs=(
            P(None, "gx", "gy"),
            P("gx", "gy"),
            P("gx", "gy", None, None),
            P("gx", "gy", None),
            P("gx", "gy", None, None),
            P("gx", "gy", None, None, None),
            P("gx", "gy", None, None),
            P("gx", "gy", None, None, None),
        ),
        out_specs=(P(None, "gx", "gy"), P(None, "gx", "gy"), P(None, "gx", "gy")),
        check_vma=False,
    )
```

profile of v0, /device:TPU:1, one launch (start us, length us, event | category | flops | bytes accessed | tf_op | source)
XLA Modules:
  0.0 377.9 jit_solution(12129984315452648051)
XLA Ops:
  0.7 1.2 copy-done
  1.9 1.3 convolution_bitcast_fusion.3
  3.4 4.4 %collective-permute-start = (f32[2,128]{1,0:T(2,128)S(1)}, f32[2,128]{1,0:T(2,128)S(1)}, u32[]{:S(2)}, u32[]{:S(2)}) collective-permute-start(f32[2,128]{1,0:T(2,128)S(1)} %fusion.94), channel_id=1, source_target_pairs={{0,1},{1,0},{2,3},{3,2},{4,5},{5,4},{6,7},{7,6},{8,9},{9,8},{10,11... | collective-permute-start | bytes 3080 | tf_op jit(solution)/shard_map/ppermute | solution.py:32
  7.7 0.9 collective-permute-done
  8.8 4.9 %collective-permute-start.1 = (f32[2,128]{1,0:T(2,128)S(1)}, f32[2,128]{1,0:T(2,128)S(1)}, u32[]{:S(2)}, u32[]{:S(2)}) collective-permute-start(f32[2,128]{1,0:T(2,128)S(1)} %fusion.86), channel_id=1, source_target_pairs={{0,2},{1,3},{2,0},{3,1},{4,6},{5,7},{6,4},{7,5},{8,10},{9,11},{10,... | collective-permute-start | bytes 3080 | tf_op jit(solution)/shard_map/ppermute | solution.py:32
  13.8 0.9 collective-permute-done.1
  14.9 8.8 %collective-permute-start.2 = (f32[2,128]{1,0:T(2,128)S(1)}, f32[2,128]{1,0:T(2,128)S(1)}, u32[]{:S(2)}, u32[]{:S(2)}) collective-permute-start(f32[2,128]{1,0:T(2,128)S(1)} %fusion.78), channel_id=1, source_target_pairs={{0,4},{1,5},{2,6},{3,7},{4,0},{5,1},{6,2},{7,3},{8,12},{9,13},{10,... | collective-permute-start | bytes 3080 | tf_op jit(solution)/shard_map/ppermute | solution.py:32
  23.7 0.9 collective-permute-done.2
  24.8 13.1 %collective-permute-start.3 = (f32[2,128]{1,0:T(2,128)S(1)}, f32[2,128]{1,0:T(2,128)S(1)}, u32[]{:S(2)}, u32[]{:S(2)}) collective-permute-start(f32[2,128]{1,0:T(2,128)S(1)} %fusion.70), channel_id=1, source_target_pairs={{0,8},{1,9},{2,10},{3,11},{4,12},{5,13},{6,14},{7,15},{8,0},{9,1},... | collective-permute-start | bytes 3080 | tf_op jit(solution)/shard_map/ppermute | solution.py:32
  37.9 0.9 collective-permute-done.3
  39.0 9.2 %collective-permute-start.4 = (f32[2,128]{1,0:T(2,128)S(1)}, f32[2,128]{1,0:T(2,128)S(1)}, u32[]{:S(2)}, u32[]{:S(2)}) collective-permute-start(f32[2,128]{1,0:T(2,128)S(1)} %fusion.62), channel_id=1, source_target_pairs={{0,16},{1,17},{2,18},{3,19},{4,20},{5,21},{6,22},{7,23},{8,24},{9,... | collective-permute-start | bytes 3080 | tf_op jit(solution)/shard_map/ppermute | solution.py:32
  49.1 1.9 collective-permute-start.5
  51.1 2.4 collective-permute-done.5
  53.6 2.5 collective-permute-start.6
  56.2 3.3 collective-permute-done.6
  59.6 1.9 collective-permute-start.7
  62.5 1.4 collective-permute-done.7
  64.1 2.5 collective-permute-start.8
  66.6 1.7 convolution_bitcast_fusion.1
  68.6 1.4 collective-permute-done.8
  74.2 1.0 convolution_add_fusion.1
  75.2 6.8 %collective-permute-start.10 = (f32[3,1,128]{2,0,1:T(4,128)S(1)}, f32[3,1,128]{2,0,1:T(4,128)S(1)}, u32[]{:S(2)}, u32[]{:S(2)}) collective-permute-start(f32[3,1,128]{2,0,1:T(4,128)S(1)} %get-tuple-element.18), channel_id=1, source_target_pairs={{16,0},{32,16},{48,32},{64,48},{80,64},{96,80},{112,96},{128,112},... | collective-permute-start | bytes 4616 | tf_op jit(solution)/shard_map/ppermute | solution.py:22
  82.0 1.9 collective-permute-start.9
  83.9 1.1 collective-permute-done.9
  85.2 1.6 collective-permute-start.11
  86.8 1.3 collective-permute-start.12
  88.1 3.4 collective-permute-done.12
  92.7 109.6 %all-reduce = (f32[2]{0:T(128)S(1)}, f32[2]{0:T(128)S(1)}) all-reduce(f32[2]{0:T(128)S(1)} %get-tuple-element.7, f32[2]{0:T(128)S(1)} %get-tuple-element.6), channel_id=1, replica_groups=mesh['gx'=32,'gy'=16] {'gx','gy'}, use_global_device_ids=true, to_apply=%region_1.0 | all-reduce | flops 4 | bytes 32 | tf_op jit(solution)/shard_map/psum | solution.py:119
  204.2 1.9 collective-permute-start.13
  206.2 2.4 collective-permute-done.13
  208.7 1.9 collective-permute-start.14
  210.6 3.3 collective-permute-done.14
  214.1 4.0 %collective-permute-start.15 = (f32[2,128]{1,0:T(2,128)S(1)}, f32[2,128]{1,0:T(2,128)S(1)}, u32[]{:S(2)}, u32[]{:S(2)}) collective-permute-start(f32[2,128]{1,0:T(2,128)S(1)} %fusion.74), channel_id=1, source_target_pairs={{0,4},{1,5},{2,6},{3,7},{4,0},{5,1},{6,2},{7,3},{8,12},{9,13},{10,... | collective-permute-start | bytes 3080 | tf_op jit(solution)/shard_map/ppermute | solution.py:32
  218.1 4.2 %collective-permute-done.15 = f32[2,128]{1,0:T(2,128)S(1)} collective-permute-done((f32[2,128]{1,0:T(2,128)S(1)}, f32[2,128]{1,0:T(2,128)S(1)}, u32[]{:S(2)}, u32[]{:S(2)}) %collective-permute-start.15) | collective-permute-done | bytes 1056 | tf_op jit(solution)/shard_map/ppermute | solution.py:32
  222.5 8.2 %collective-permute-start.16 = (f32[2,128]{1,0:T(2,128)S(1)}, f32[2,128]{1,0:T(2,128)S(1)}, u32[]{:S(2)}, u32[]{:S(2)}) collective-permute-start(f32[2,128]{1,0:T(2,128)S(1)} %fusion.66), channel_id=1, source_target_pairs={{0,8},{1,9},{2,10},{3,11},{4,12},{5,13},{6,14},{7,15},{8,0},{9,1},... | collective-permute-start | bytes 3080 | tf_op jit(solution)/shard_map/ppermute | solution.py:32
  230.7 4.8 %collective-permute-done.16 = f32[2,128]{1,0:T(2,128)S(1)} collective-permute-done((f32[2,128]{1,0:T(2,128)S(1)}, f32[2,128]{1,0:T(2,128)S(1)}, u32[]{:S(2)}, u32[]{:S(2)}) %collective-permute-start.16) | collective-permute-done | bytes 1056 | tf_op jit(solution)/shard_map/ppermute | solution.py:32
  236.0 7.7 %collective-permute-start.17 = (f32[2,128]{1,0:T(2,128)S(1)}, f32[2,128]{1,0:T(2,128)S(1)}, u32[]{:S(2)}, u32[]{:S(2)}) collective-permute-start(f32[2,128]{1,0:T(2,128)S(1)} %fusion.58), channel_id=1, source_target_pairs={{0,16},{1,17},{2,18},{3,19},{4,20},{5,21},{6,22},{7,23},{8,24},{9,... | collective-permute-start | bytes 3080 | tf_op jit(solution)/shard_map/ppermute | solution.py:32
  245.1 1.9 collective-permute-start.18
  247.0 2.4 collective-permute-done.18
  250.0 2.5 collective-permute-start.19
  252.5 3.3 collective-permute-done.19
  256.3 1.9 collective-permute-start.20
  258.5 2.2 collective-permute-done.20
  261.6 2.8 collective-permute-start.21
  264.3 1.7 convolution_bitcast_fusion
  267.7 0.9 convolution_add_fusion.10
  273.5 1.1 multiply_reduce_fusion
  274.6 101.4 %psum.23 = f32[2]{0:T(128)S(1)} all-reduce(f32[2]{0:T(128)S(1)} %get-tuple-element.21), channel_id=1, replica_groups=mesh['gx'=32,'gy'=16] {'gx','gy'}, use_global_device_ids=true, to_apply=%region_5.0 | all-reduce | flops 2 | bytes 16 | tf_op jit(solution)/shard_map/psum | solution.py:126
  (126 shorter events, 23.7 us)
Async XLA Ops:
  0.6 1.2 copy-start
  0.6 2.5 copy-start.4
  0.7 8.0 %copy-start.1 = (f32[1,1,8,128,128]{4,3,2,1,0:T(8,128)S(1)}, f32[1,1,8,128,128]{4,3,2,1,0:T(8,128)}, u32[]{:S(2)}) copy-start(f32[1,1,8,128,128]{4,3,2,1,0:T(8,128)} %param.13) | copy-start | bytes 1572868
  0.7 65.9 %copy-start.2 = (f32[4,4,128,128]{3,2,1,0:T(8,128)S(1)}, f32[4,4,128,128]{3,2,1,0:T(8,128)}, u32[]{:S(2)}) copy-start(f32[4,4,128,128]{3,2,1,0:T(8,128)} %param.10) | copy-start | bytes 3145732
  3.4 5.3 %collective-permute-start = (f32[2,128]{1,0:T(2,128)S(1)}, f32[2,128]{1,0:T(2,128)S(1)}, u32[]{:S(2)}, u32[]{:S(2)}) collective-permute-start(f32[2,128]{1,0:T(2,128)S(1)} %fusion.94), channel_id=1, source_target_pairs={{0,1},{1,0},{2,3},{3,2},{4,5},{5,4},{6,7},{7,6},{8,9},{9,8},{10,11... | collective-permute-start | bytes 3080 | tf_op jit(solution)/shard_map/ppermute | solution.py:32
  8.8 5.9 %collective-permute-start.1 = (f32[2,128]{1,0:T(2,128)S(1)}, f32[2,128]{1,0:T(2,128)S(1)}, u32[]{:S(2)}, u32[]{:S(2)}) collective-permute-start(f32[2,128]{1,0:T(2,128)S(1)} %fusion.86), channel_id=1, source_target_pairs={{0,2},{1,3},{2,0},{3,1},{4,6},{5,7},{6,4},{7,5},{8,10},{9,11},{10,... | collective-permute-start | bytes 3080 | tf_op jit(solution)/shard_map/ppermute | solution.py:32
  14.9 9.8 %collective-permute-start.2 = (f32[2,128]{1,0:T(2,128)S(1)}, f32[2,128]{1,0:T(2,128)S(1)}, u32[]{:S(2)}, u32[]{:S(2)}) collective-permute-start(f32[2,128]{1,0:T(2,128)S(1)} %fusion.78), channel_id=1, source_target_pairs={{0,4},{1,5},{2,6},{3,7},{4,0},{5,1},{6,2},{7,3},{8,12},{9,13},{10,... | collective-permute-start | bytes 3080 | tf_op jit(solution)/shard_map/ppermute | solution.py:32
  24.8 14.0 %collective-permute-start.3 = (f32[2,128]{1,0:T(2,128)S(1)}, f32[2,128]{1,0:T(2,128)S(1)}, u32[]{:S(2)}, u32[]{:S(2)}) collective-permute-start(f32[2,128]{1,0:T(2,128)S(1)} %fusion.70), channel_id=1, source_target_pairs={{0,8},{1,9},{2,10},{3,11},{4,12},{5,13},{6,14},{7,15},{8,0},{9,1},... | collective-permute-start | bytes 3080 | tf_op jit(solution)/shard_map/ppermute | solution.py:32
  39.0 10.0 %collective-permute-start.4 = (f32[2,128]{1,0:T(2,128)S(1)}, f32[2,128]{1,0:T(2,128)S(1)}, u32[]{:S(2)}, u32[]{:S(2)}) collective-permute-start(f32[2,128]{1,0:T(2,128)S(1)} %fusion.62), channel_id=1, source_target_pairs={{0,16},{1,17},{2,18},{3,19},{4,20},{5,21},{6,22},{7,23},{8,24},{9,... | collective-permute-start | bytes 3080 | tf_op jit(solution)/shard_map/ppermute | solution.py:32
  49.1 4.3 %collective-permute-start.5 = (f32[2,128]{1,0:T(2,128)S(1)}, f32[2,128]{1,0:T(2,128)S(1)}, u32[]{:S(2)}, u32[]{:S(2)}) collective-permute-start(f32[2,128]{1,0:T(2,128)S(1)} %fusion.54), channel_id=1, source_target_pairs={{0,32},{1,33},{2,34},{3,35},{4,36},{5,37},{6,38},{7,39},{8,40},{9,... | collective-permute-start | bytes 3080 | tf_op jit(solution)/shard_map/ppermute | solution.py:32
  53.6 5.8 %collective-permute-start.6 = (f32[2,128]{1,0:T(2,128)S(1)}, f32[2,128]{1,0:T(2,128)S(1)}, u32[]{:S(2)}, u32[]{:S(2)}) collective-permute-start(f32[2,128]{1,0:T(2,128)S(1)} %fusion.46), channel_id=1, source_target_pairs={{0,64},{1,65},{2,66},{3,67},{4,68},{5,69},{6,70},{7,71},{8,72},{9,... | collective-permute-start | bytes 3080 | tf_op jit(solution)/shard_map/ppermute | solution.py:32
  59.6 4.3 %collective-permute-start.7 = (f32[2,128]{1,0:T(2,128)S(1)}, f32[2,128]{1,0:T(2,128)S(1)}, u32[]{:S(2)}, u32[]{:S(2)}) collective-permute-start(f32[2,128]{1,0:T(2,128)S(1)} %fusion.38), channel_id=1, source_target_pairs={{0,128},{1,129},{2,130},{3,131},{4,132},{5,133},{6,134},{7,135},{8... | collective-permute-start | bytes 3080 | tf_op jit(solution)/shard_map/ppermute | solution.py:32
  64.1 6.0 %copy-start.3 = (f32[1,1,9,128,128]{4,3,2,1,0:T(8,128)S(1)}, f32[1,1,9,128,128]{4,3,2,1,0:T(8,128)}, u32[]{:S(2)}) copy-start(f32[1,1,9,128,128]{4,3,2,1,0:T(8,128)} %param.15) | copy-start | bytes 1769476
  64.1 6.0 %collective-permute-start.8 = (f32[2,128]{1,0:T(2,128)S(1)}, f32[2,128]{1,0:T(2,128)S(1)}, u32[]{:S(2)}, u32[]{:S(2)}) collective-permute-start(f32[2,128]{1,0:T(2,128)S(1)} %fusion.30), channel_id=1, source_target_pairs={{0,256},{1,257},{2,258},{3,259},{4,260},{5,261},{6,262},{7,263},{8... | collective-permute-start | bytes 3080 | tf_op jit(solution)/shard_map/ppermute | solution.py:32
  73.1 0.9 copy-start.6
  74.2 1.0 copy-start.7
  75.2 8.8 %collective-permute-start.10 = (f32[3,1,128]{2,0,1:T(4,128)S(1)}, f32[3,1,128]{2,0,1:T(4,128)S(1)}, u32[]{:S(2)}, u32[]{:S(2)}) collective-permute-start(f32[3,1,128]{2,0,1:T(4,128)S(1)} %get-tuple-element.18), channel_id=1, source_target_pairs={{16,0},{32,16},{48,32},{64,48},{80,64},{96,80},{112,96},{128,112},... | collective-permute-start | bytes 4616 | tf_op jit(solution)/shard_map/ppermute | solution.py:22
  82.0 3.1 collective-permute-start.9
  85.2 3.0 collective-permute-start.11
  86.8 4.7 %collective-permute-start.12 = (f32[3,18,1]{2,0,1:T(4,128)S(1)}, f32[3,18,1]{2,0,1:T(4,128)S(1)}, u32[]{:S(2)}, u32[]{:S(2)}) collective-permute-start(f32[3,18,1]{2,0,1:T(4,128)S(1)} %get-tuple-element.11), channel_id=1, source_target_pairs={{1,0},{2,1},{3,2},{4,3},{5,4},{6,5},{7,6},{8,7},{9,8},{10,9},{11,1... | collective-permute-start | bytes 656 | tf_op jit(solution)/shard_map/ppermute | solution.py:22
  91.7 0.7 copy-start.5
  202.3 0.6 copy-start.18
  202.9 0.5 copy-start.16
  204.2 4.3 %collective-permute-start.13 = (f32[2,128]{1,0:T(2,128)S(1)}, f32[2,128]{1,0:T(2,128)S(1)}, u32[]{:S(2)}, u32[]{:S(2)}) collective-permute-start(f32[2,128]{1,0:T(2,128)S(1)} %fusion.90), channel_id=1, source_target_pairs={{0,1},{1,0},{2,3},{3,2},{4,5},{5,4},{6,7},{7,6},{8,9},{9,8},{10,11... | collective-permute-start | bytes 3080 | tf_op jit(solution)/shard_map/ppermute | solution.py:32
  208.7 5.2 %collective-permute-start.14 = (f32[2,128]{1,0:T(2,128)S(1)}, f32[2,128]{1,0:T(2,128)S(1)}, u32[]{:S(2)}, u32[]{:S(2)}) collective-permute-start(f32[2,128]{1,0:T(2,128)S(1)} %fusion.82), channel_id=1, source_target_pairs={{0,2},{1,3},{2,0},{3,1},{4,6},{5,7},{6,4},{7,5},{8,10},{9,11},{10,... | collective-permute-start | bytes 3080 | tf_op jit(solution)/shard_map/ppermute | solution.py:32
  214.1 8.2 %collective-permute-start.15 = (f32[2,128]{1,0:T(2,128)S(1)}, f32[2,128]{1,0:T(2,128)S(1)}, u32[]{:S(2)}, u32[]{:S(2)}) collective-permute-start(f32[2,128]{1,0:T(2,128)S(1)} %fusion.74), channel_id=1, source_target_pairs={{0,4},{1,5},{2,6},{3,7},{4,0},{5,1},{6,2},{7,3},{8,12},{9,13},{10,... | collective-permute-start | bytes 3080 | tf_op jit(solution)/shard_map/ppermute | solution.py:32
  222.5 13.0 %collective-permute-start.16 = (f32[2,128]{1,0:T(2,128)S(1)}, f32[2,128]{1,0:T(2,128)S(1)}, u32[]{:S(2)}, u32[]{:S(2)}) collective-permute-start(f32[2,128]{1,0:T(2,128)S(1)} %fusion.66), channel_id=1, source_target_pairs={{0,8},{1,9},{2,10},{3,11},{4,12},{5,13},{6,14},{7,15},{8,0},{9,1},... | collective-permute-start | bytes 3080 | tf_op jit(solution)/shard_map/ppermute | solution.py:32
  235.5 0.5 copy-start.8
  236.0 8.5 %collective-permute-start.17 = (f32[2,128]{1,0:T(2,128)S(1)}, f32[2,128]{1,0:T(2,128)S(1)}, u32[]{:S(2)}, u32[]{:S(2)}) collective-permute-start(f32[2,128]{1,0:T(2,128)S(1)} %fusion.58), channel_id=1, source_target_pairs={{0,16},{1,17},{2,18},{3,19},{4,20},{5,21},{6,22},{7,23},{8,24},{9,... | collective-permute-start | bytes 3080 | tf_op jit(solution)/shard_map/ppermute | solution.py:32
  244.5 0.6 copy-start.10
  245.1 4.3 %collective-permute-start.18 = (f32[2,128]{1,0:T(2,128)S(1)}, f32[2,128]{1,0:T(2,128)S(1)}, u32[]{:S(2)}, u32[]{:S(2)}) collective-permute-start(f32[2,128]{1,0:T(2,128)S(1)} %fusion.50), channel_id=1, source_target_pairs={{0,32},{1,33},{2,34},{3,35},{4,36},{5,37},{6,38},{7,39},{8,40},{9,... | collective-permute-start | bytes 3080 | tf_op jit(solution)/shard_map/ppermute | solution.py:32
  249.4 0.6 copy-start.12
  250.0 5.8 %collective-permute-start.19 = (f32[2,128]{1,0:T(2,128)S(1)}, f32[2,128]{1,0:T(2,128)S(1)}, u32[]{:S(2)}, u32[]{:S(2)}) collective-permute-start(f32[2,128]{1,0:T(2,128)S(1)} %fusion.42), channel_id=1, source_target_pairs={{0,64},{1,65},{2,66},{3,67},{4,68},{5,69},{6,70},{7,71},{8,72},{9,... | collective-permute-start | bytes 3080 | tf_op jit(solution)/shard_map/ppermute | solution.py:32
  255.8 0.6 copy-start.14
  256.3 4.4 %collective-permute-start.20 = (f32[2,128]{1,0:T(2,128)S(1)}, f32[2,128]{1,0:T(2,128)}, u32[]{:S(2)}, u32[]{:S(2)}) collective-permute-start(f32[2,128]{1,0:T(2,128)S(1)} %fusion.34), channel_id=1, source_target_pairs={{0,128},{1,129},{2,130},{3,131},{4,132},{5,133},{6,134},{7,135},{8... | collective-permute-start | bytes 3080 | tf_op jit(solution)/shard_map/ppermute | solution.py:32
  261.6 5.8 %collective-permute-start.21 = (f32[2,128]{1,0:T(2,128)S(1)}, f32[2,128]{1,0:T(2,128)S(1)}, u32[]{:S(2)}, u32[]{:S(2)}) collective-permute-start(f32[2,128]{1,0:T(2,128)S(1)} %fusion.26), channel_id=1, source_target_pairs={{0,256},{1,257},{2,258},{3,259},{4,260},{5,261},{6,262},{7,263},{8... | collective-permute-start | bytes 3080 | tf_op jit(solution)/shard_map/ppermute | solution.py:32
  268.6 0.7 copy-start.15
  269.4 0.7 copy-start.13
  270.3 0.7 copy-start.11
  271.1 0.7 copy-start.9
  274.6 101.4 %copy-start.19 = (f32[2]{0:T(128)S(1)}, f32[2]{0:T(128)}, u32[]{:S(2)}) copy-start(f32[2]{0:T(128)} %copy-done.18) | copy-start | bytes 28
  376.0 0.6 copy-start.17
where the time goes:
time: 379 us; the launch traced here: 378 us
  blocking collectives  211 us (56%)
  starting transfers between devices  93.8 us (25%)
  waiting for transfers between devices  41.5 us (11%)
  matrix products  18.7 us (5%)
  local copies, waits for them, and re-layouts  11.2 us (3%)
    psum x1, blocking collectives, on_device(): rz_old = lax.psum(local_rz, ('gx', 'gy'))  110 us
    psum x1, blocking collectives, on_device(): rz_new = lax.psum(jnp.sum(residual * second_z, axis=(1, 2)), ('gx', 'gy'))  101 us
    ppermute x18, starting transfers between devices, from_partner(): return lax.ppermute(value, axis, pairs)  82.1 us
    ppermute x18, waiting for transfers between devices, from_partner(): return lax.ppermute(value, axis, pairs)  37 us
    unnamed x44, local copies, waits for them, and re-layouts  9.48 us
    ppermute x2, starting transfers between devices, extended(): lax.ppermute(head, axis, [((i + 1) % count, i) for i in range(ends)])  8.12 us
  transfers between devices with their start and end apart: 22, of which 20 were waited for; matrix products, arithmetic and copies ran while one was open for 2% of the time, Pallas kernels for 0%

commit v1 on v0

--- a/solution.py
+++ b/solution.py
@@ -116,7 +116,7 @@
     )
     first_z = apply_inverse(right_side)
     local_rz = jnp.sum(right_side * first_z, axis=(1, 2))
-    rz_old = lax.psum(local_rz, ("gx", "gy"))
+    rz_old = lax.psum(lax.psum(local_rz, "gy"), "gx")
     applied = stencil(first_z, conductivity)
     curvature = lax.psum(jnp.sum(first_z * applied, axis=(1, 2)), ("gx", "gy"))
     step_size = (rz_old / curvature)[:, None, None]

time: 379 us -> 468 us (1.23)
  blocking collectives: 211 us -> 300 us
  waiting for transfers between devices: 41.5 us -> 36.3 us
  starting transfers between devices: 93.8 us -> 98.8 us
    psum x1 -> x3, blocking collectives: 110 us -> 196 us  [the longest x1 98.8 us: on_device(): curvature = lax.psum(jnp.sum(first_z * applied, axis=(1, 2)), ('gx', 'gy'))]
    ppermute x18, waiting for transfers between devices: 37 us -> 31.8 us  [from_partner(): return lax.ppermute(value, axis, pairs)]
    ppermute x18, starting transfers between devices: 82.1 us -> 87.1 us  [from_partner(): return lax.ppermute(value, axis, pairs)]
  transfers between devices with their start and end apart: 22 -> 22, of which waited for: 20 -> 20; matrix products, arithmetic and copies ran while one was open for 2% -> 1% of each run, Pallas kernels for 0% -> 0%
where the time goes in v1:
time: 468 us; the launch traced here: 467 us
  blocking collectives  300 us (64%)
  starting transfers between devices  98.8 us (21%)
  waiting for transfers between devices  36.3 us (8%)
  matrix products  18.6 us (4%)
  local copies, waits for them, and re-layouts  10.9 us (2%)
    psum x1, blocking collectives, on_device(): rz_new = lax.psum(jnp.sum(residual * second_z, axis=(1, 2)), ('gx', 'gy'))  104 us
    psum x1, blocking collectives, on_device(): curvature = lax.psum(jnp.sum(first_z * applied, axis=(1, 2)), ('gx', 'gy'))  98.8 us
    psum x2, blocking collectives, on_device(): rz_old = lax.psum(lax.psum(local_rz, 'gy'), 'gx')  97.7 us
    ppermute x18, starting transfers between devices, from_partner(): return lax.ppermute(value, axis, pairs)  87.1 us
    ppermute x18, waiting for transfers between devices, from_partner(): return lax.ppermute(value, axis, pairs)  31.8 us
  transfers between devices with their start and end apart: 22, of which 20 were waited for; matrix products, arithmetic and copies ran while one was open for 1% of the time, Pallas kernels for 0%

profile of v1, /device:TPU:1, one launch (start us, length us, event | category | flops | bytes accessed | tf_op | source)
XLA Modules:
  0.0 466.7 jit_solution(892643002577639793)
XLA Ops:
  0.7 1.2 copy-done
  1.9 1.3 convolution_bitcast_fusion.3
  3.4 4.4 collective-permute-start
  7.7 0.9 collective-permute-done
  8.8 4.9 %collective-permute-start.1 = (f32[2,128]{1,0:T(2,128)S(1)}, f32[2,128]{1,0:T(2,128)S(1)}, u32[]{:S(2)}, u32[]{:S(2)}) collective-permute-start(f32[2,128]{1,0:T(2,128)S(1)} %fusion.86), channel_id=1, source_target_pairs={{0,2},{1,3},{2,0},{3,1},{4,6},{5,7},{6,4},{7,5},{8,10},{9,11},{10,... | collective-permute-start | bytes 3080 | tf_op jit(solution)/shard_map/ppermute | solution.py:32
  13.8 0.9 collective-permute-done.1
  14.9 8.8 %collective-permute-start.2 = (f32[2,128]{1,0:T(2,128)S(1)}, f32[2,128]{1,0:T(2,128)S(1)}, u32[]{:S(2)}, u32[]{:S(2)}) collective-permute-start(f32[2,128]{1,0:T(2,128)S(1)} %fusion.78), channel_id=1, source_target_pairs={{0,4},{1,5},{2,6},{3,7},{4,0},{5,1},{6,2},{7,3},{8,12},{9,13},{10,... | collective-permute-start | bytes 3080 | tf_op jit(solution)/shard_map/ppermute | solution.py:32
  23.7 0.9 collective-permute-done.2
  24.8 13.1 %collective-permute-start.3 = (f32[2,128]{1,0:T(2,128)S(1)}, f32[2,128]{1,0:T(2,128)S(1)}, u32[]{:S(2)}, u32[]{:S(2)}) collective-permute-start(f32[2,128]{1,0:T(2,128)S(1)} %fusion.70), channel_id=1, source_target_pairs={{0,8},{1,9},{2,10},{3,11},{4,12},{5,13},{6,14},{7,15},{8,0},{9,1},... | collective-permute-start | bytes 3080 | tf_op jit(solution)/shard_map/ppermute | solution.py:32
  37.9 0.9 collective-permute-done.3
  39.0 9.2 %collective-permute-start.4 = (f32[2,128]{1,0:T(2,128)S(1)}, f32[2,128]{1,0:T(2,128)S(1)}, u32[]{:S(2)}, u32[]{:S(2)}) collective-permute-start(f32[2,128]{1,0:T(2,128)S(1)} %fusion.62), channel_id=1, source_target_pairs={{0,16},{1,17},{2,18},{3,19},{4,20},{5,21},{6,22},{7,23},{8,24},{9,... | collective-permute-start | bytes 3080 | tf_op jit(solution)/shard_map/ppermute | solution.py:32
  49.1 1.9 collective-permute-start.5
  51.1 2.4 collective-permute-done.5
  53.6 2.5 collective-permute-start.6
  56.2 3.3 collective-permute-done.6
  59.6 1.9 collective-permute-start.7
  62.5 1.4 collective-permute-done.7
  64.1 2.5 collective-permute-start.8
  66.6 1.7 convolution_bitcast_fusion.1
  68.6 1.4 collective-permute-done.8
  74.2 1.0 convolution_add_fusion.1
  75.2 6.8 %collective-permute-start.10 = (f32[3,1,128]{2,0,1:T(4,128)S(1)}, f32[3,1,128]{2,0,1:T(4,128)S(1)}, u32[]{:S(2)}, u32[]{:S(2)}) collective-permute-start(f32[3,1,128]{2,0,1:T(4,128)S(1)} %get-tuple-element.16), channel_id=1, source_target_pairs={{16,0},{32,16},{48,32},{64,48},{80,64},{96,80},{112,96},{128,112},... | collective-permute-start | bytes 4616 | tf_op jit(solution)/shard_map/ppermute | solution.py:22
  82.0 1.9 collective-permute-start.9
  83.9 1.1 collective-permute-done.9
  85.2 1.6 collective-permute-start.11
  86.8 1.3 collective-permute-start.12
  88.1 3.4 collective-permute-done.12
  92.7 26.3 %psum.28 = f32[2]{0:T(128)S(1)} all-reduce(f32[2]{0:T(128)S(1)} %get-tuple-element.7), channel_id=1, replica_groups=mesh['gx'=32,'gy'=16] {'gy'}, use_global_device_ids=true, to_apply=%region_1.0 | all-reduce | flops 2 | bytes 16 | tf_op jit(solution)/shard_map/psum | solution.py:119
  119.0 71.3 %psum.29 = f32[2]{0:T(128)S(1)} all-reduce(f32[2]{0:T(128)S(1)} %psum.28), channel_id=1, replica_groups=mesh['gx'=32,'gy'=16] {'gx'}, use_global_device_ids=true, to_apply=%region_2.0 | all-reduce | flops 2 | bytes 16 | tf_op jit(solution)/shard_map/psum | solution.py:119
  190.4 98.8 %psum.30 = f32[2]{0:T(128)S(1)} all-reduce(f32[2]{0:T(128)S(1)} %get-tuple-element.6), channel_id=1, replica_groups=mesh['gx'=32,'gy'=16] {'gx','gy'}, use_global_device_ids=true, to_apply=%region_4.0 | all-reduce | flops 2 | bytes 16 | tf_op jit(solution)/shard_map/psum | solution.py:121
  290.6 3.7 collective-permute-start.13
  295.4 3.0 collective-permute-start.14
  298.4 2.2 collective-permute-done.14
  300.8 5.1 %collective-permute-start.15 = (f32[2,128]{1,0:T(2,128)S(1)}, f32[2,128]{1,0:T(2,128)S(1)}, u32[]{:S(2)}, u32[]{:S(2)}) collective-permute-start(f32[2,128]{1,0:T(2,128)S(1)} %fusion.74), channel_id=1, source_target_pairs={{0,4},{1,5},{2,6},{3,7},{4,0},{5,1},{6,2},{7,3},{8,12},{9,13},{10,... | collective-permute-start | bytes 3080 | tf_op jit(solution)/shard_map/ppermute | solution.py:32
  305.9 3.1 collective-permute-done.15
  309.2 9.3 %collective-permute-start.16 = (f32[2,128]{1,0:T(2,128)S(1)}, f32[2,128]{1,0:T(2,128)S(1)}, u32[]{:S(2)}, u32[]{:S(2)}) collective-permute-start(f32[2,128]{1,0:T(2,128)S(1)} %fusion.66), channel_id=1, source_target_pairs={{0,8},{1,9},{2,10},{3,11},{4,12},{5,13},{6,14},{7,15},{8,0},{9,1},... | collective-permute-start | bytes 3080 | tf_op jit(solution)/shard_map/ppermute | solution.py:32
  318.5 3.7 collective-permute-done.16
  322.8 7.2 %collective-permute-start.17 = (f32[2,128]{1,0:T(2,128)S(1)}, f32[2,128]{1,0:T(2,128)S(1)}, u32[]{:S(2)}, u32[]{:S(2)}) collective-permute-start(f32[2,128]{1,0:T(2,128)S(1)} %fusion.58), channel_id=1, source_target_pairs={{0,16},{1,17},{2,18},{3,19},{4,20},{5,21},{6,22},{7,23},{8,24},{9,... | collective-permute-start | bytes 3080 | tf_op jit(solution)/shard_map/ppermute | solution.py:32
  331.4 1.9 collective-permute-start.18
  333.3 2.4 collective-permute-done.18
  336.2 2.7 collective-permute-start.19
  338.9 3.1 collective-permute-done.19
  342.6 1.9 collective-permute-start.20
  344.8 2.2 collective-permute-done.20
  347.8 3.0 collective-permute-start.21
  350.8 1.7 convolution_bitcast_fusion
  359.8 1.1 multiply_reduce_fusion
  360.9 103.7 %psum.31 = f32[2]{0:T(128)S(1)} all-reduce(f32[2]{0:T(128)S(1)} %get-tuple-element.19), channel_id=1, replica_groups=mesh['gx'=32,'gy'=16] {'gx','gy'}, use_global_device_ids=true, to_apply=%region_6.0 | all-reduce | flops 2 | bytes 16 | tf_op jit(solution)/shard_map/psum | solution.py:126
  (128 shorter events, 25.0 us)
Async XLA Ops:
  0.6 1.2 copy-start
  0.6 2.5 copy-start.4
  0.7 8.0 %copy-start.1 = (f32[1,1,8,128,128]{4,3,2,1,0:T(8,128)S(1)}, f32[1,1,8,128,128]{4,3,2,1,0:T(8,128)}, u32[]{:S(2)}) copy-start(f32[1,1,8,128,128]{4,3,2,1,0:T(8,128)} %param.13) | copy-start | bytes 1572868
  0.7 65.9 %copy-start.2 = (f32[4,4,128,128]{3,2,1,0:T(8,128)S(1)}, f32[4,4,128,128]{3,2,1,0:T(8,128)}, u32[]{:S(2)}) copy-start(f32[4,4,128,128]{3,2,1,0:T(8,128)} %param.10) | copy-start | bytes 3145732
  3.4 5.3 %collective-permute-start = (f32[2,128]{1,0:T(2,128)S(1)}, f32[2,128]{1,0:T(2,128)S(1)}, u32[]{:S(2)}, u32[]{:S(2)}) collective-permute-start(f32[2,128]{1,0:T(2,128)S(1)} %fusion.94), channel_id=1, source_target_pairs={{0,1},{1,0},{2,3},{3,2},{4,5},{5,4},{6,7},{7,6},{8,9},{9,8},{10,11... | collective-permute-start | bytes 3080 | tf_op jit(solution)/shard_map/ppermute | solution.py:32
  8.8 5.9 %collective-permute-start.1 = (f32[2,128]{1,0:T(2,128)S(1)}, f32[2,128]{1,0:T(2,128)S(1)}, u32[]{:S(2)}, u32[]{:S(2)}) collective-permute-start(f32[2,128]{1,0:T(2,128)S(1)} %fusion.86), channel_id=1, source_target_pairs={{0,2},{1,3},{2,0},{3,1},{4,6},{5,7},{6,4},{7,5},{8,10},{9,11},{10,... | collective-permute-start | bytes 3080 | tf_op jit(solution)/shard_map/ppermute | solution.py:32
  14.9 9.8 %collective-permute-start.2 = (f32[2,128]{1,0:T(2,128)S(1)}, f32[2,128]{1,0:T(2,128)S(1)}, u32[]{:S(2)}, u32[]{:S(2)}) collective-permute-start(f32[2,128]{1,0:T(2,128)S(1)} %fusion.78), channel_id=1, source_target_pairs={{0,4},{1,5},{2,6},{3,7},{4,0},{5,1},{6,2},{7,3},{8,12},{9,13},{10,... | collective-permute-start | bytes 3080 | tf_op jit(solution)/shard_map/ppermute | solution.py:32
  24.8 14.0 %collective-permute-start.3 = (f32[2,128]{1,0:T(2,128)S(1)}, f32[2,128]{1,0:T(2,128)S(1)}, u32[]{:S(2)}, u32[]{:S(2)}) collective-permute-start(f32[2,128]{1,0:T(2,128)S(1)} %fusion.70), channel_id=1, source_target_pairs={{0,8},{1,9},{2,10},{3,11},{4,12},{5,13},{6,14},{7,15},{8,0},{9,1},... | collective-permute-start | bytes 3080 | tf_op jit(solution)/shard_map/ppermute | solution.py:32
  39.0 10.0 %collective-permute-start.4 = (f32[2,128]{1,0:T(2,128)S(1)}, f32[2,128]{1,0:T(2,128)S(1)}, u32[]{:S(2)}, u32[]{:S(2)}) collective-permute-start(f32[2,128]{1,0:T(2,128)S(1)} %fusion.62), channel_id=1, source_target_pairs={{0,16},{1,17},{2,18},{3,19},{4,20},{5,21},{6,22},{7,23},{8,24},{9,... | collective-permute-start | bytes 3080 | tf_op jit(solution)/shard_map/ppermute | solution.py:32
  49.1 4.3 collective-permute-start.5
  53.6 5.8 %collective-permute-start.6 = (f32[2,128]{1,0:T(2,128)S(1)}, f32[2,128]{1,0:T(2,128)S(1)}, u32[]{:S(2)}, u32[]{:S(2)}) collective-permute-start(f32[2,128]{1,0:T(2,128)S(1)} %fusion.46), channel_id=1, source_target_pairs={{0,64},{1,65},{2,66},{3,67},{4,68},{5,69},{6,70},{7,71},{8,72},{9,... | collective-permute-start | bytes 3080 | tf_op jit(solution)/shard_map/ppermute | solution.py:32
  59.6 4.3 collective-permute-start.7
  64.1 6.0 %copy-start.3 = (f32[1,1,9,128,128]{4,3,2,1,0:T(8,128)S(1)}, f32[1,1,9,128,128]{4,3,2,1,0:T(8,128)}, u32[]{:S(2)}) copy-start(f32[1,1,9,128,128]{4,3,2,1,0:T(8,128)} %param.15) | copy-start | bytes 1769476
  64.1 6.0 %collective-permute-start.8 = (f32[2,128]{1,0:T(2,128)S(1)}, f32[2,128]{1,0:T(2,128)S(1)}, u32[]{:S(2)}, u32[]{:S(2)}) collective-permute-start(f32[2,128]{1,0:T(2,128)S(1)} %fusion.30), channel_id=1, source_target_pairs={{0,256},{1,257},{2,258},{3,259},{4,260},{5,261},{6,262},{7,263},{8... | collective-permute-start | bytes 3080 | tf_op jit(solution)/shard_map/ppermute | solution.py:32
  73.1 0.9 copy-start.6
  74.2 1.0 copy-start.7
  75.2 8.8 %collective-permute-start.10 = (f32[3,1,128]{2,0,1:T(4,128)S(1)}, f32[3,1,128]{2,0,1:T(4,128)S(1)}, u32[]{:S(2)}, u32[]{:S(2)}) collective-permute-start(f32[3,1,128]{2,0,1:T(4,128)S(1)} %get-tuple-element.16), channel_id=1, source_target_pairs={{16,0},{32,16},{48,32},{64,48},{80,64},{96,80},{112,96},{128,112},... | collective-permute-start | bytes 4616 | tf_op jit(solution)/shard_map/ppermute | solution.py:22
  82.0 3.1 collective-permute-start.9
  85.2 3.0 collective-permute-start.11
  86.8 4.7 %collective-permute-start.12 = (f32[3,18,1]{2,0,1:T(4,128)S(1)}, f32[3,18,1]{2,0,1:T(4,128)S(1)}, u32[]{:S(2)}, u32[]{:S(2)}) collective-permute-start(f32[3,18,1]{2,0,1:T(4,128)S(1)} %get-tuple-element.9), channel_id=1, source_target_pairs={{1,0},{2,1},{3,2},{4,3},{5,4},{6,5},{7,6},{8,7},{9,8},{10,9},{11,1... | collective-permute-start | bytes 656 | tf_op jit(solution)/shard_map/ppermute | solution.py:22
  91.7 0.7 copy-start.5
  190.4 98.8 %copy-start.18 = (f32[2]{0:T(128)}, f32[2]{0:T(128)S(1)}, u32[]{:S(2)}) copy-start(f32[2]{0:T(128)S(1)} %psum.29) | copy-start | bytes 28
  289.2 0.6 copy-start.16
  290.6 4.6 collective-permute-start.13
  295.4 5.2 %collective-permute-start.14 = (f32[2,128]{1,0:T(2,128)S(1)}, f32[2,128]{1,0:T(2,128)S(1)}, u32[]{:S(2)}, u32[]{:S(2)}) collective-permute-start(f32[2,128]{1,0:T(2,128)S(1)} %fusion.82), channel_id=1, source_target_pairs={{0,2},{1,3},{2,0},{3,1},{4,6},{5,7},{6,4},{7,5},{8,10},{9,11},{10,... | collective-permute-start | bytes 3080 | tf_op jit(solution)/shard_map/ppermute | solution.py:32
  300.8 8.2 %collective-permute-start.15 = (f32[2,128]{1,0:T(2,128)S(1)}, f32[2,128]{1,0:T(2,128)S(1)}, u32[]{:S(2)}, u32[]{:S(2)}) collective-permute-start(f32[2,128]{1,0:T(2,128)S(1)} %fusion.74), channel_id=1, source_target_pairs={{0,4},{1,5},{2,6},{3,7},{4,0},{5,1},{6,2},{7,3},{8,12},{9,13},{10,... | collective-permute-start | bytes 3080 | tf_op jit(solution)/shard_map/ppermute | solution.py:32
  309.2 13.0 %collective-permute-start.16 = (f32[2,128]{1,0:T(2,128)S(1)}, f32[2,128]{1,0:T(2,128)S(1)}, u32[]{:S(2)}, u32[]{:S(2)}) collective-permute-start(f32[2,128]{1,0:T(2,128)S(1)} %fusion.66), channel_id=1, source_target_pairs={{0,8},{1,9},{2,10},{3,11},{4,12},{5,13},{6,14},{7,15},{8,0},{9,1},... | collective-permute-start | bytes 3080 | tf_op jit(solution)/shard_map/ppermute | solution.py:32
  322.2 0.6 copy-start.8
  322.8 8.0 %collective-permute-start.17 = (f32[2,128]{1,0:T(2,128)S(1)}, f32[2,128]{1,0:T(2,128)S(1)}, u32[]{:S(2)}, u32[]{:S(2)}) collective-permute-start(f32[2,128]{1,0:T(2,128)S(1)} %fusion.58), channel_id=1, source_target_pairs={{0,16},{1,17},{2,18},{3,19},{4,20},{5,21},{6,22},{7,23},{8,24},{9,... | collective-permute-start | bytes 3080 | tf_op jit(solution)/shard_map/ppermute | solution.py:32
  330.8 0.6 copy-start.10
  331.4 4.3 collective-permute-start.18
  335.7 0.6 copy-start.12
  336.2 5.8 %collective-permute-start.19 = (f32[2,128]{1,0:T(2,128)S(1)}, f32[2,128]{1,0:T(2,128)S(1)}, u32[]{:S(2)}, u32[]{:S(2)}) collective-permute-start(f32[2,128]{1,0:T(2,128)S(1)} %fusion.42), channel_id=1, source_target_pairs={{0,64},{1,65},{2,66},{3,67},{4,68},{5,69},{6,70},{7,71},{8,72},{9,... | collective-permute-start | bytes 3080 | tf_op jit(solution)/shard_map/ppermute | solution.py:32
  342.0 0.6 copy-start.14
  342.6 4.4 collective-permute-start.20
  347.8 5.8 %collective-permute-start.21 = (f32[2,128]{1,0:T(2,128)S(1)}, f32[2,128]{1,0:T(2,128)S(1)}, u32[]{:S(2)}, u32[]{:S(2)}) collective-permute-start(f32[2,128]{1,0:T(2,128)S(1)} %fusion.26), channel_id=1, source_target_pairs={{0,256},{1,257},{2,258},{3,259},{4,260},{5,261},{6,262},{7,263},{8... | collective-permute-start | bytes 3080 | tf_op jit(solution)/shard_map/ppermute | solution.py:32
  354.8 0.7 copy-start.15
  355.7 0.7 copy-start.13
  356.5 0.7 copy-start.11
  357.4 0.7 copy-start.9
  360.9 103.8 %copy-start.19 = (f32[2]{0:T(128)S(1)}, f32[2]{0:T(128)}, u32[]{:S(2)}) copy-start(f32[2]{0:T(128)} %copy-done.18) | copy-start | bytes 28
  464.7 0.7 copy-start.17
